TPU v7x, 32 devices: a whole 2x2x4 slice. The times are simulated.
32 devices in a mesh: grp: 2 (over core), mem: 16 (over z, y, x).
Axes of the slice: x: 2, y: 2, z: 4, core: 2. Of those that a mesh axis runs over, the one named last changes fastest.
Arguments:
- spectra: bfloat16 [256, 2, 16, 512], P(('grp', 'mem')), may hold values from -40 to 40
- partners: int32 [1, 16], replicated, may hold values from 0 to 1, as said below
Outputs:
- correlations: bfloat16 [256, 1, 128, 513], P(('grp', 'mem'))
Inputs may be any that keep to these rules, and one draw needn't show every extreme that they name: For each member index k the offsets partners[r, k] of the rounds are distinct (offset 0 pairs a block with its own group).
All inputs are finite; a program needn't handle non-finite values.
Results may differ from a plain program's by a relative error of at most 0.0068.
Values may be sent and summed in bfloat16 or wider, within the bound.
A program may use at most 128 MiB of HBM per device.

v0:
```python
import math

import jax
import jax.numpy as jnp
from jax import lax
from jax.sharding import PartitionSpec as P

SMOOTH = 32


def from_partner(array, axis, distance):
    return lax.ppermute(array, axis, [(i, i ^ 1 << distance) for i in range(lax.axis_size(axis))])


def whiten(spectra, half_width):
    components = spectra.astype(jnp.float32)
    power_sum = components[:, 0] * components[:, 0] + components[:, 1] * components[:, 1]
    bin_count = power_sum.shape[-1]
    positions = jnp.arange(bin_count, dtype=jnp.int32)
    band_matrix = (jnp.abs(positions[:, None] - positions[None, :]) <= half_width).astype(
        jnp.float32
    )
    smooth = jnp.dot(power_sum.reshape(-1, bin_count), band_matrix, precision=lax.Precision.HIGHEST)
    smooth = smooth.reshape(power_sum.shape) / (2 * half_width + 1)
    inv_level = lax.rsqrt(smooth + 1e-05)
    return (components * inv_level[:, None]).astype(jnp.bfloat16)


def lag_table(bin_count):
    centre = bin_count // 2
    frequency = jnp.arange(bin_count, dtype=jnp.int32)[:, None]
    lag_offset = jnp.arange(bin_count + 1, dtype=jnp.int32)[None, :] - centre
    angles = jnp.mod(frequency * lag_offset, 2 * bin_count).astype(jnp.float32) * (
        math.pi / bin_count
    )
    return jnp.stack([jnp.cos(angles), -jnp.sin(angles)], 0).astype(jnp.bfloat16)


def pair_lags(own_block, partner_block, transform):
    factor = math.sqrt(2.0 / (own_block.shape[3] * own_block.shape[2]))
    rotated = jnp.stack([own_block, jnp.stack([own_block[:, 1], -own_block[:, 0]], 1)], 0)
    cross_spectra = jnp.einsum(
        "oicsf,jcsf->ofij", rotated, partner_block, preferred_element_type=jnp.float32
    ).astype(jnp.bfloat16)
    lag_sums = jnp.einsum(
        "ofij,ofl->ijl", cross_spectra, transform, preferred_element_type=jnp.float32
    )
    return (lag_sums * factor).astype(jnp.bfloat16)


def correlate_piece(own_block, transform, received):
    return pair_lags(own_block, received, transform)


def route_shard(payload, offset, levels):
    for level in range(levels):
        swapped = from_partner(payload, "grp", level)
        payload = jnp.where(offset // 2**level % 2 == 1, swapped, payload)
    return payload


def on_device(spectra, partners):
    whitened = whiten(spectra, SMOOTH)
    transform = lag_table(spectra.shape[3])
    rounds = partners.shape[0]
    member_index = lax.axis_index("mem")
    levels = lax.axis_size("grp").bit_length() - 1
    outputs = []
    for round_index in range(rounds):
        own_offset = partners[round_index, member_index]
        source = route_shard(whitened, own_offset, levels)
        outputs.append(
            correlate_piece(whitened, transform, lax.all_gather(source, "mem", axis=0, tiled=True))
        )
    return jnp.stack(outputs, 1)


def solution(mesh):
    placed = (P(("grp", "mem"), None, None, None), P())
    return jax.shard_map(
        on_device,
        mesh=mesh,
        in_specs=placed,
        out_specs=P(("grp", "mem"), None, None, None),
        check_vma=False,
    )
```

profile of v0, /device:TPU:0, one launch (start us, length us, event | category | flops | bytes accessed | tf_op | source)
XLA Modules:
  0.0 113.8 jit_solution(16226402458105554186)
XLA Ops:
  6.5 0.0 copy-start
  6.5 0.0 copy-start.1
  6.5 0.0 all-gather.2.cloned.1.call-start
  6.5 1.1 convert_element_type.33
  7.6 0.5 fusion.10
  8.1 0.0 copy-done.1
  8.1 0.1 multiply_convert_fusion
  8.2 0.5 collective-permute-start
  8.7 0.0 copy-done
  8.7 0.6 constant_dynamic-slice_fusion
  11.2 0.0 collective-permute-done
  11.2 0.8 broadcast_select_fusion
  12.0 0.0 all-gather.2.cloned.1.call-update
  12.1 0.1 fusion.31
  12.2 0.1 pad_maximum_fusion
  12.2 6.5 %copy.6 = bf16[2,8,2,16,512]{3,1,2,0,4:T(8,128)(2,1)} copy(bf16[2,8,2,16,512]{4,3,2,1,0:T(8,128)(2,1)S(1)} %pad_maximum_fusion) | data formatting | bytes 1048576 | tf_op jit(solution)/shard_map/stack | solution.py:41
  18.7 4.7 %cosine_convert_fusion = (bf16[1,512,513]{1,2,0:T(8,128)(2,1)S(1)}, bf16[1,512,513]{1,2,0:T(8,128)(2,1)S(1)}) fusion(s32[513]{0:T(1024)S(1)} %iota_add_fusion), kind=kLoop, calls=%fused_computation.19 | loop fusion | flops 4465152 | bytes 1052676 | tf_op jit(solution)/shard_map/convert
  23.4 67.3 %all-gather.2.cloned.1.call-done = bf16[128,2,16,512]{3,2,1,0:T(8,128)(2,1)} async-done(((bf16[8,2,16,512]{3,2,1,0:T(8,128)(2,1)}), bf16[128,2,16,512]{3,2,1,0:T(8,128)(2,1)}) %all-gather.2.cloned.1.call-update) | async-done | bytes 4194320 | tf_op jit(solution)/shard_map/all_gather | solution.py:73
  90.7 9.1 %copy.5 = bf16[128,2,16,512,1]{0,2,1,4,3:T(8,128)(2,1)} copy(bf16[128,2,16,512,1]{3,2,1,0,4:T(8,128)(2,1)} %bitcast.42) | data formatting | bytes 8388608 | tf_op jit(solution)/shard_map/all_gather | solution.py:73
  99.9 4.7 %fusion.28 = bf16[512,128,2,8,1]{1,3,4,2,0:T(8,128)(2,1)S(1)} fusion(bf16[128,2,16,512,1]{0,2,1,4,3:T(8,128)(2,1)} %copy.5, bf16[2,8,2,16,512]{3,1,2,0,4:T(8,128)(2,1)} %copy.6), kind=kOutput, calls=%fused_computation.40 | convolution fusion | flops 67108864 | bytes 6815744 | tf_op jit(solution)/shard_map/oicsf,jcsf->ofij/dot_general | solution.py:42
  104.6 1.3 %fusion.6 = bf16[8,1,128,513]{2,3,0,1:T(8,128)(2,1)S(1)} fusion(bf16[512,128,2,8,1]{1,3,4,2,0:T(8,128)(2,1)S(1)} %fusion.28, bf16[1,512,513]{1,2,0:T(8,128)(2,1)S(1)} %get-tuple-element.8, bf16[1,512,513]{1,2,0:T(8,128)(2,1)S(1)} %get-tuple-element.7), kind=kOutput, calls=%fused_computation.8 | convolution fusion | flops 1077414912 | bytes 4198400 | tf_op jit(solution)/shard_map/ofij,ofl->ijl/dot_general | solution.py:45
  105.9 1.1 copy.4
  (3 shorter events, 0.1 us)
Async XLA Ops:
  6.5 2.1 %copy-start = (s32[1,16]{1,0:T(1,128)S(1)}, s32[1,16]{1,0:T(1,128)}, u32[]{:S(2)}) copy-start(s32[1,16]{1,0:T(1,128)} %param.3) | copy-start | bytes 196
  6.5 1.5 %copy-start.1 = (bf16[8,2,16,512]{3,2,1,0:T(8,128)(2,1)S(1)}, bf16[8,2,16,512]{3,2,1,0:T(8,128)(2,1)}, u32[]{:S(2)}) copy-start(bf16[8,2,16,512]{3,2,1,0:T(8,128)(2,1)} %param.2) | copy-start | bytes 786436
  6.5 84.2 %all-gather.2.cloned.1.call-start = ((), (), s32[]{:S(2)}) async-start(), calls=%async_computation | async-start | bytes 4456448 | tf_op jit(solution)/shard_map/all_gather | solution.py:73
  8.2 3.1 %collective-permute-start = (bf16[8,2,16,512]{3,2,1,0:T(8,128)(2,1)S(1)}, bf16[8,2,16,512]{3,2,1,0:T(8,128)(2,1)S(1)}, u32[]{:S(2)}, u32[]{:S(2)}) collective-permute-start(bf16[8,2,16,512]{3,2,1,0:T(8,128)(2,1)S(1)} %multiply_convert_fusion), channel_id=1, source_target_pairs={{0,16},{16,0},{1,17},{17,1},{2,18},{18,2},{3,19},{19,3},{4,20},{20... | collective-permute-start | bytes 786440 | tf_op jit(solution)/shard_map/ppermute | solution.py:12
Sparse Core Ops, SparseCore 0:
  12.2 78.4 all-gather.1
where the time goes:
time: 114 us
  waiting for transfers between devices  67.3 us (59%)
  local copies, waits for them, and re-layouts  17.3 us (15%)
  between operations  15.4 us (14%)
  other arithmetic  6.8 us (6%)
  matrix products  6.45 us (6%)
    all_gather x1, waiting for transfers between devices, on_device(): lax.all_gather(source, 'mem', axis=0, tiled=True)  67.3 us
    all_gather x1, local copies, waits for them, and re-layouts, on_device(): lax.all_gather(source, 'mem', axis=0, tiled=True)  9.15 us
    another operation x1, local copies, waits for them, and re-layouts, pair_lags(): jnp.stack([own_block, jnp.stack([own_block[:, 1], -own_block[:, 0]], 1)], 0)  6.47 us
    dot_general x1, matrix products, pair_lags(): jnp.einsum('oicsf,jcsf->ofij', rotated, partner_block, preferred_element_...  4.72 us
    another operation x1, other arithmetic  4.72 us
  transfers between devices with their start and end apart: 2, of which 1 were waited for; matrix products, arithmetic and copies ran while one was open for 10% of the time, Pallas kernels for 0%

commit v1 on v0

v1 whole, which is shorter than its diff:
```python
import functools
import math

import jax
import jax.numpy as jnp
import numpy as np
from jax import lax
from jax.experimental import pallas as pl
from jax.experimental.pallas import tpu as pltpu
from jax.sharding import PartitionSpec as P

SMOOTH = 32
FLOOR = 1e-05
MESH = pl.DeviceIdType.MESH

NZ = 4
CHUNKS = 2
OVER_XY = {0: (0, 1), 1: (1, 2), 2: (1, 2), 3: (2, 3)}
OWN, XCOL, YCOL, DIAG = (0, 0), (1, 0), (0, 1), (1, 1)


def from_partner(array, axis, distance):
    return lax.ppermute(array, axis, [(i, i ^ 1 << distance) for i in range(lax.axis_size(axis))])


def whiten(spectra, half_width):
    components = spectra.astype(jnp.float32)
    power_sum = components[:, 0] * components[:, 0] + components[:, 1] * components[:, 1]
    bin_count = power_sum.shape[-1]
    positions = jnp.arange(bin_count, dtype=jnp.int32)
    band_matrix = (jnp.abs(positions[:, None] - positions[None, :]) <= half_width).astype(
        jnp.float32
    )
    smooth = jnp.dot(power_sum.reshape(-1, bin_count), band_matrix, precision=lax.Precision.HIGHEST)
    smooth = smooth.reshape(power_sum.shape) / (2 * half_width + 1)
    inv_level = lax.rsqrt(smooth + FLOOR)
    return (components * inv_level[:, None]).astype(jnp.bfloat16)


def lag_table(bin_count):
    frequency = np.arange(bin_count)[:, None]
    lag_offset = np.arange(bin_count + 1)[None, :] - bin_count // 2
    angles = np.mod(frequency * lag_offset, 2 * bin_count) * (math.pi / bin_count)
    return np.stack([np.cos(angles), -np.sin(angles)], 0).astype(jnp.bfloat16)


def pair_lags(own_block, partner_block, transform):
    factor = math.sqrt(2.0 / (own_block.shape[3] * own_block.shape[2]))
    rotated = jnp.stack([own_block, jnp.stack([own_block[:, 1], -own_block[:, 0]], 1)], 0)
    cross_spectra = jnp.einsum(
        "oicsf,jcsf->ofij", rotated, partner_block, preferred_element_type=jnp.float32
    ).astype(jnp.bfloat16)
    lag_sums = jnp.einsum(
        "ofij,ofl->ijl", cross_spectra, transform, preferred_element_type=jnp.float32
    )
    return (lag_sums * factor).astype(jnp.bfloat16)


def route_shard(payload, offset, levels):
    for level in range(levels):
        swapped = from_partner(payload, "grp", level)
        payload = jnp.where(offset // 2**level % 2 == 1, swapped, payload)
    return payload


def any_mesh(spectra, partners):
    whitened = whiten(spectra, SMOOTH)
    transform = jnp.asarray(lag_table(spectra.shape[3]))
    member_index = lax.axis_index("mem")
    levels = lax.axis_size("grp").bit_length() - 1
    outputs = []
    for round_index in range(partners.shape[0]):
        source = route_shard(whitened, partners[round_index, member_index], levels)
        gathered = lax.all_gather(source, "mem", axis=0, tiled=True)
        outputs.append(pair_lags(whitened, gathered, transform))
    return jnp.stack(outputs, 1)


def forwards(z, column, plane, chunk):
    links = []
    if column == OWN:
        if plane >= z and z > 0:
            links.append("down")
        if plane <= z and z < NZ - 1:
            links.append("up")
        links += ["x", "y"]
    elif column == XCOL:
        if plane in OVER_XY[z] and chunk < CHUNKS // 2:
            links.append("y")
    elif column == YCOL:
        if plane in OVER_XY[z] and chunk >= CHUNKS // 2:
            links.append("x")
    else:
        if z > 0 and plane >= z and plane not in OVER_XY[z - 1]:
            links.append("down")
        if z < NZ - 1 and plane <= z and plane not in OVER_XY[z + 1]:
            links.append("up")
    return links


def arrivals():
    order = {z: [] for z in range(NZ)}
    waiting = {(z, link): [] for z in range(NZ) for link in ("up", "down", "x", "y")}

    def take(z, piece):
        for link in forwards(z, *piece):
            waiting[z, link].append(piece)

    for z in range(NZ):
        for chunk in range(CHUNKS):
            take(z, (OWN, z, chunk))
    while any(waiting.values()):
        landed = []
        for (z, link), queue in waiting.items():
            if queue:
                (dx, dy), plane, chunk = queue.pop(0)
                if link == "x":
                    landed.append((z, ((1 - dx, dy), plane, chunk)))
                elif link == "y":
                    landed.append((z, ((dx, 1 - dy), plane, chunk)))
                else:
                    step = 1 if link == "up" else -1
                    landed.append((z + step, ((dx, dy), plane, chunk)))
        for z, piece in landed:
            order[z].append(piece)
            take(z, piece)
    return order


def plan():
    steps = {}
    for z, pieces in arrivals().items():
        have = {(dy, plane): 0 for dy in (0, 1) for plane in range(NZ)}
        have[0, z] = CHUNKS
        steps[z], taken = [], []
        for piece in pieces:
            (dx, dy), plane, _ = piece
            taken.append(piece)
            have[dy, plane] += 1
            if have[dy, plane] == 2 * CHUNKS:
                steps[z].append((taken, plane * 2 + dy))
                taken = []
        assert not taken and len(steps[z]) == 2 * NZ
    return steps


def slice_kernel(
    partners_ref, spectra_ref, table_ref, out_ref,
    whole, bright, mine, mate, gathered, cross, send_sem, recv_sem, mate_send, mate_recv,
):
    channels, _, segments, bins = spectra_ref.shape
    lags = out_ref.shape[3]
    rows = segments * 2 * channels
    part = rows // CHUNKS
    grp, me = lax.axis_index("grp"), lax.axis_index("mem")
    x, y, z = me % 2, me // 2 % 2, me // 4
    target = {
        "x": (grp, me + 1 - 2 * x),
        "y": (grp, me + 2 - 4 * y),
        "up": (grp, me + 4),
        "down": (grp, me - 4),
        "mate": (1 - grp, me),
    }
    lane = {"x": 0, "y": 1, "up": 2, "down": 3}

    barrier = pltpu.get_barrier_semaphore()

    def greet(name):
        pl.semaphore_signal(barrier, inc=1, device_id=target[name], device_id_type=MESH)

    for name in ("mate", "x", "y"):
        greet(name)
    pl.when(z > 0)(lambda: greet("down"))
    pl.when(z < NZ - 1)(lambda: greet("up"))

    first = lax.broadcasted_iota(jnp.int32, (bins, bins), 0)
    second = lax.broadcasted_iota(jnp.int32, (bins, bins), 1)
    band = jnp.where(jnp.abs(first - second) <= SMOOTH, 1.0, 0.0).astype(jnp.bfloat16)
    values = spectra_ref[...].astype(jnp.float32)
    power = values[:, 0] * values[:, 0] + values[:, 1] * values[:, 1]
    power = power.reshape(channels * segments, bins)
    high = power.astype(jnp.bfloat16)
    low = (power - high.astype(jnp.float32)).astype(jnp.bfloat16)
    smooth = jnp.dot(high, band, preferred_element_type=jnp.float32)
    smooth += jnp.dot(low, band, preferred_element_type=jnp.float32)
    inverse = lax.rsqrt(smooth * (1.0 / (2 * SMOOTH + 1)) + FLOOR)
    inverse = inverse.reshape(channels, segments, bins)
    for channel in range(channels):
        for k in range(2):
            row = k * channels + channel
            white = spectra_ref[channel, k].astype(jnp.float32) * inverse[channel]
            for tile in range(bins // 128):
                at = pl.ds(row, segments, stride=2 * channels)
                whole[tile, at, :] = white[:, tile * 128 : (tile + 1) * 128]
    for tile in range(bins // 128):
        mine[:, tile * 128 : (tile + 1) * 128] = whole[tile].astype(jnp.bfloat16)

    pl.semaphore_wait(barrier, 3 + jnp.where(z > 0, 1, 0) + jnp.where(z < NZ - 1, 1, 0))

    def to_mate(chunk):
        piece = pl.ds(chunk * part, part)
        return pltpu.make_async_remote_copy(
            src_ref=mine.at[piece], dst_ref=mate.at[piece],
            send_sem=mate_send.at[chunk], recv_sem=mate_recv.at[chunk],
            device_id=target["mate"], device_id_type=MESH,
        )

    def member(column, plane):
        dx, dy = column
        return plane * 4 + (y if dy == 0 else 1 - y) * 2 + (x if dx == 0 else 1 - x)

    def copy(link, column, plane, chunk):
        slot = member(column, plane)
        piece = gathered.at[slot, pl.ds(chunk * part, part)]
        return pltpu.make_async_remote_copy(
            src_ref=piece, dst_ref=piece,
            send_sem=send_sem.at[lane[link], slot, chunk], recv_sem=recv_sem.at[slot, chunk],
            device_id=target[link], device_id_type=MESH,
        )

    def pass_on(zc, column, plane, chunk):
        for link in forwards(zc, column, plane, chunk):
            copy(link, column, plane, chunk).start()

    for chunk in range(CHUNKS):
        to_mate(chunk).start()
    other = partners_ref[0, me] % 2 == 1
    for chunk in range(CHUNKS):
        to_mate(chunk).wait_recv()
        piece = pl.ds(chunk * part, part)
        gathered[me, piece] = jnp.where(other, mate[piece], mine[piece])
        for zc in range(NZ):
            pl.when(z == zc)(functools.partial(pass_on, zc, OWN, zc, chunk))

    @pl.loop(0, segments)
    def _(segment):
        block = mine[pl.ds(pl.multiple_of(segment * 2 * channels, 16), 2 * channels)]
        block = block.astype(jnp.float32)
        for row in range(2 * channels):
            bright[segment, row] = jnp.broadcast_to(block[row : row + 1], (8, bins))

    steps = plan()
    factor = math.sqrt(2.0 / (bins * segments))

    def take(zc, pieces):
        for column, plane, chunk in pieces:
            copy("x", column, plane, chunk).wait_recv()
            pass_on(zc, column, plane, chunk)

    packed = 0
    for zc in range(NZ):
        number = sum(code * 8**index for index, (_, code) in enumerate(steps[zc]))
        packed = jnp.where(z == zc, number, packed)

    def step(index, packed):
        for zc in range(NZ):
            @pl.when(z == zc)
            def _():
                for number, (pieces, _) in enumerate(steps[zc]):
                    if pieces:
                        pl.when(index == number)(functools.partial(take, zc, pieces))

        code = packed % 8
        plane, dy = code // 2, code % 2
        pair = plane * 2 + y + dy - 2 * y * dy

        @pl.loop(0, bins // 128)
        def _(tile):
            lanes = pl.ds(pl.multiple_of(tile * 128, 128), 128)

            def add(segment, sums):
                sums = list(sums)
                at = pl.ds(pl.multiple_of(segment * 2 * channels, 16), 2 * channels)
                theirs = []
                for side in range(2):
                    block = gathered[pair * 2 + side, at, lanes].astype(jnp.float32)
                    theirs.append((block[:channels], block[channels:]))
                for i in range(channels):
                    real = bright[segment, i, :, lanes]
                    imag = bright[segment, channels + i, :, lanes]
                    for side, (b_real, b_imag) in enumerate(theirs):
                        at_sum = (i * 2 + side) * 2
                        sums[at_sum] += real * b_real + imag * b_imag
                        sums[at_sum + 1] += imag * b_real - real * b_imag
                return tuple(sums)

            zeros = tuple(jnp.zeros((8, 128), jnp.float32) for _ in range(4 * channels))
            sums = lax.fori_loop(0, segments, add, zeros)
            for i in range(channels):
                for o in range(2):
                    both = jnp.concatenate([sums[i * 4 + o], sums[i * 4 + 2 + o]], 0)
                    at = pl.ds(pl.multiple_of(tile * 128 + o * bins, 128), 128)
                    cross[i * 16 : (i + 1) * 16, at] = both.astype(jnp.bfloat16)

        result = jnp.dot(cross[...], table_ref[...], preferred_element_type=jnp.float32)
        result = (result * factor).astype(jnp.bfloat16)
        at = pl.ds(pl.multiple_of(pair * 16, 16), 16)
        for i in range(channels):
            out_ref[i, 0, at, :] = result[i * 16 : (i + 1) * 16, :lags]
        return packed // 8

    lax.fori_loop(0, 2 * NZ, step, packed)

    for chunk in range(CHUNKS):
        to_mate(chunk).wait_send()

    def drain(zc):
        pieces = [(OWN, zc, chunk) for chunk in range(CHUNKS)]
        pieces += [piece for taken, _ in steps[zc] for piece in taken]
        for piece in pieces:
            for link in forwards(zc, *piece):
                copy(link, *piece).wait_send()

    for zc in range(NZ):
        pl.when(z == zc)(functools.partial(drain, zc))


def on_slice(spectra, partners):
    channels, _, segments, bins = spectra.shape
    members = lax.axis_size("mem")
    rows = segments * 2 * channels
    lags = bins + 1
    wide = -(-lags // 128) * 128
    table = np.zeros((2 * bins, wide), jnp.bfloat16)
    table[:, :lags] = lag_table(bins).reshape(2 * bins, lags)
    vmem = pl.BlockSpec(memory_space=pltpu.VMEM)
    return pl.pallas_call(
        slice_kernel,
        out_shape=jax.ShapeDtypeStruct((channels, 1, members * channels, lags), jnp.bfloat16),
        in_specs=[pl.BlockSpec(memory_space=pltpu.SMEM), vmem, vmem],
        out_specs=vmem,
        scratch_shapes=[
            pltpu.VMEM((bins // 128, rows, 128), jnp.float32),
            pltpu.VMEM((segments, 2 * channels, 8, bins), jnp.float32),
            pltpu.VMEM((rows, bins), jnp.bfloat16),
            pltpu.VMEM((rows, bins), jnp.bfloat16),
            pltpu.VMEM((members, rows, bins), jnp.bfloat16),
            pltpu.VMEM((16 * channels, 2 * bins), jnp.bfloat16),
            pltpu.SemaphoreType.DMA((4, members, CHUNKS)),
            pltpu.SemaphoreType.DMA((members, CHUNKS)),
            pltpu.SemaphoreType.DMA((CHUNKS,)),
            pltpu.SemaphoreType.DMA((CHUNKS,)),
        ],
        compiler_params=pltpu.CompilerParams(
            collective_id=0, has_side_effects=True, vmem_limit_bytes=48 * 2**20
        ),
        cost_estimate=pl.CostEstimate(
            flops=2 * channels * members * channels * 2 * bins * lags,
            bytes_accessed=4 * 2**20,
            transcendentals=0,
        ),
    )(partners, spectra, jnp.asarray(table))


def solution(mesh):
    shape = (mesh.shape["grp"], mesh.shape["mem"])

    def on_device(spectra, partners):
        fits = spectra.shape == (8, 2, 16, 512) and partners.shape[0] == 1
        if shape == (2, 4 * NZ) and fits:
            return on_slice(spectra, partners)
        return any_mesh(spectra, partners)

    return jax.shard_map(
        on_device,
        mesh=mesh,
        in_specs=(P(("grp", "mem"), None, None, None), P()),
        out_specs=P(("grp", "mem"), None, None, None),
        check_vma=False,
    )
```

time: 114 us -> 54.5 us (0.48)
  waiting for transfers between devices: 67.3 us -> 0 us
  Pallas kernels: 0 us -> 48.9 us
  between operations: 15.4 us -> 0.01 us
  local copies, waits for them, and re-layouts: 17.3 us -> 4.73 us
  other arithmetic: 6.8 us -> 0 us
  matrix products: 6.45 us -> 0 us
    all_gather x1 -> x0, waiting for transfers between devices: 67.3 us -> none  [on_device(): lax.all_gather(source, 'mem', axis=0, tiled=True)]
    pallas_call x0 -> x1, Pallas kernels: none -> 48.9 us  [on_slice(): pl.pallas_call(slice_kernel, out_shape=jax.ShapeDtypeStruct((channels, 1,...]
    all_gather x1 -> x0, local copies, waits for them, and re-layouts: 9.15 us -> none  [on_device(): lax.all_gather(source, 'mem', axis=0, tiled=True)]
    another operation x2 -> x0, local copies, waits for them, and re-layouts: 7.57 us -> none  [the longest x1 6.47 us: pair_lags(): jnp.stack([own_block, jnp.stack([own_block[:, 1], -own_block[:, 0]], 1)], 0)]
    dot_general x3 -> x0, matrix products: 6.45 us -> none  [the longest x1 4.72 us: pair_lags(): jnp.einsum('oicsf,jcsf->ofij', rotated, partner_block, preferred_element_...]
    another operation x4 -> x0, other arithmetic: 4.85 us -> none
    unnamed x4 -> x6, local copies, waits for them, and re-layouts: 0.01 us -> 2.92 us
    pallas_call x0 -> x1, local copies, waits for them, and re-layouts: none -> 1.81 us  [on_slice(): pl.pallas_call(slice_kernel, out_shape=jax.ShapeDtypeStruct((channels, 1,...]
  transfers between devices with their start and end apart: 2 -> 0, of which waited for: 1 -> 0; matrix products, arithmetic and copies ran while one was open for 10% -> 0% of each run, Pallas kernels for 0% -> 0%
where the time goes in v1:
time: 54.5 us; the launch traced here: 53.7 us
  Pallas kernels  48.9 us (90%)
  local copies, waits for them, and re-layouts  4.73 us (9%)
    pallas_call x1, Pallas kernels, on_slice(): pl.pallas_call(slice_kernel, out_shape=jax.ShapeDtypeStruct((channels, 1,...  48.9 us
    unnamed x6, local copies, waits for them, and re-layouts  2.92 us
    pallas_call x1, local copies, waits for them, and re-layouts, on_slice(): pl.pallas_call(slice_kernel, out_shape=jax.ShapeDtypeStruct((channels, 1,...  1.81 us

profile of v1, /device:TPU:0, one launch (start us, length us, event | category | flops | bytes accessed | tf_op | source)
XLA Modules:
  0.0 53.7 jit_solution(3626233559214819377)
XLA Ops:
  0.0 0.0 copy-start
  0.0 0.9 %copy-done = bf16[8,2,16,512]{3,2,1,0:T(8,128)(2,1)S(1)} copy-done((bf16[8,2,16,512]{3,2,1,0:T(8,128)(2,1)S(1)}, bf16[8,2,16,512]{3,2,1,0:T(8,128)(2,1)}, u32[]{:S(2)}) %copy-start) | copy-done | bytes 262168
  1.0 0.0 copy-start.1
  1.0 0.7 %copy-done.1 = s32[1,16]{1,0:T(1,128)S(1)} copy-done((s32[1,16]{1,0:T(1,128)S(1)}, s32[1,16]{1,0:T(1,128)}, u32[]{:S(2)}) %copy-start.1) | copy-done | bytes 88
  1.6 0.0 copy-start.2
  1.6 1.3 %copy-done.2 = bf16[1024,640]{1,0:T(8,128)(2,1)S(1)} copy-done((bf16[1024,640]{1,0:T(8,128)(2,1)S(1)}, bf16[1024,640]{1,0:T(8,128)(2,1)}, u32[]{:S(2)}) %copy-start.2) | copy-done | bytes 1310744
  2.9 48.9 %shard_map.37 = bf16[8,1,128,513]{3,2,1,0:T(8,128)(2,1)S(1)} custom-call(s32[1,16]{1,0:T(1,128)S(1)} %copy-done.1, bf16[8,2,16,512]{3,2,1,0:T(8,128)(2,1)S(1)} %copy-done, bf16[1024,640]{1,0:T(8,128)(2,1)S(1)} %copy-done.2), custom_call_target="tpu_custom_call" | custom-call | flops 1075838976 | bytes 4194304 | tf_op jit(solution)/shard_map/pallas_call | solution.py:327
  51.9 1.8 %copy.4 = bf16[8,1,128,513]{2,0,3,1:T(8,128)(2,1)} copy(bf16[8,1,128,513]{3,2,1,0:T(8,128)(2,1)S(1)} %shard_map.37) | data formatting | bytes 2101248 | tf_op jit(solution)/shard_map/pallas_call | solution.py:327
Async XLA Ops:
  0.0 0.9 %copy-start = (bf16[8,2,16,512]{3,2,1,0:T(8,128)(2,1)S(1)}, bf16[8,2,16,512]{3,2,1,0:T(8,128)(2,1)}, u32[]{:S(2)}) copy-start(bf16[8,2,16,512]{3,2,1,0:T(8,128)(2,1)} %spectra_ref.1) | copy-start | bytes 786436
  1.0 0.7 %copy-start.1 = (s32[1,16]{1,0:T(1,128)S(1)}, s32[1,16]{1,0:T(1,128)}, u32[]{:S(2)}) copy-start(s32[1,16]{1,0:T(1,128)} %partners_ref.1) | copy-start | bytes 196
  1.6 1.3 %copy-start.2 = (bf16[1024,640]{1,0:T(8,128)(2,1)S(1)}, bf16[1024,640]{1,0:T(8,128)(2,1)}, u32[]{:S(2)}) copy-start(bf16[1024,640]{1,0:T(8,128)(2,1)} %constant.2.clone.table_ref) | copy-start | bytes 3932164

commit v2 on v1

--- a/solution.py
+++ b/solution.py
@@ -14,7 +14,9 @@
 MESH = pl.DeviceIdType.MESH
 
 NZ = 4
-CHUNKS = 2
+CHUNKS = 4
+TILES = 4
+SEND_TICKS, HOP_TICKS, TAKE_TICKS, TILE_TICKS, LAG_TICKS = 15, 8, 1, 4, 4
 OVER_XY = {0: (0, 1), 1: (1, 2), 2: (1, 2), 3: (2, 3)}
 OWN, XCOL, YCOL, DIAG = (0, 0), (1, 0), (0, 1), (1, 1)
 
@@ -98,49 +100,60 @@
     return links
 
 
-def arrivals():
-    order = {z: [] for z in range(NZ)}
-    waiting = {(z, link): [] for z in range(NZ) for link in ("up", "down", "x", "y")}
-
-    def take(z, piece):
+def plan():
+    links = {(z, link): [] for z in range(NZ) for link in ("up", "down", "x", "y")}
+    landed = {z: [] for z in range(NZ)}
+    have = {z: {(dy, plane): 0 for dy in (0, 1) for plane in range(NZ)} for z in range(NZ)}
+    ready = {z: [] for z in range(NZ)}
+    steps = {z: [] for z in range(NZ)}
+    taken = {z: [] for z in range(NZ)}
+    free = dict.fromkeys(range(NZ), 0)
+
+    def take(z, piece, now):
+        (_, dy), plane, _ = piece
         for link in forwards(z, *piece):
-            waiting[z, link].append(piece)
+            links[z, link].append([piece, SEND_TICKS, now])
+        have[z][dy, plane] += 1
+        if have[z][dy, plane] == 2 * CHUNKS:
+            ready[z].append((plane * 2 + dy, 0))
 
     for z in range(NZ):
         for chunk in range(CHUNKS):
-            take(z, (OWN, z, chunk))
-    while any(waiting.values()):
-        landed = []
-        for (z, link), queue in waiting.items():
-            if queue:
-                (dx, dy), plane, chunk = queue.pop(0)
-                if link == "x":
-                    landed.append((z, ((1 - dx, dy), plane, chunk)))
-                elif link == "y":
-                    landed.append((z, ((dx, 1 - dy), plane, chunk)))
+            take(z, (OWN, z, chunk), 0)
+    now = 0
+    while any(len(done) < 2 * NZ or len(done[-1][1]) < TILES for done in steps.values()):
+        for (z, link), queue in links.items():
+            if queue and queue[0][2] <= now:
+                queue[0][1] -= 1
+                if queue[0][1] == 0:
+                    (dx, dy), plane, chunk = queue.pop(0)[0]
+                    if link == "x":
+                        landed[z].append(((1 - dx, dy), plane, chunk, now + HOP_TICKS))
+                    elif link == "y":
+                        landed[z].append(((dx, 1 - dy), plane, chunk, now + HOP_TICKS))
+                    else:
+                        there = z + (1 if link == "up" else -1)
+                        landed[there].append(((dx, dy), plane, chunk, now + HOP_TICKS))
+        for z in range(NZ):
+            if free[z] > now:
+                continue
+            if landed[z] and landed[z][0][3] <= now:
+                piece = landed[z].pop(0)[:3]
+                taken[z].append(piece)
+                take(z, piece, now + TAKE_TICKS)
+                free[z] = now + TAKE_TICKS
+            elif ready[z]:
+                code, tile = ready[z].pop(0)
+                if tile == 0:
+                    steps[z].append((code, []))
+                steps[z][-1][1].append(taken[z])
+                taken[z] = []
+                free[z] = now + TILE_TICKS
+                if tile + 1 < TILES:
+                    ready[z].insert(0, (code, tile + 1))
                 else:
-                    step = 1 if link == "up" else -1
-                    landed.append((z + step, ((dx, dy), plane, chunk)))
-        for z, piece in landed:
-            order[z].append(piece)
-            take(z, piece)
-    return order
-
-
-def plan():
-    steps = {}
-    for z, pieces in arrivals().items():
-        have = {(dy, plane): 0 for dy in (0, 1) for plane in range(NZ)}
-        have[0, z] = CHUNKS
-        steps[z], taken = [], []
-        for piece in pieces:
-            (dx, dy), plane, _ = piece
-            taken.append(piece)
-            have[dy, plane] += 1
-            if have[dy, plane] == 2 * CHUNKS:
-                steps[z].append((taken, plane * 2 + dy))
-                taken = []
-        assert not taken and len(steps[z]) == 2 * NZ
+                    free[z] += LAG_TICKS
+        now += 1
     return steps
 
 
@@ -249,24 +262,23 @@
 
     packed = 0
     for zc in range(NZ):
-        number = sum(code * 8**index for index, (_, code) in enumerate(steps[zc]))
+        number = sum(code * 8**index for index, (code, _) in enumerate(steps[zc]))
         packed = jnp.where(z == zc, number, packed)
 
     def step(index, packed):
-        for zc in range(NZ):
-            @pl.when(z == zc)
-            def _():
-                for number, (pieces, _) in enumerate(steps[zc]):
-                    if pieces:
-                        pl.when(index == number)(functools.partial(take, zc, pieces))
-
         code = packed % 8
         plane, dy = code // 2, code % 2
         pair = plane * 2 + y + dy - 2 * y * dy
 
-        @pl.loop(0, bins // 128)
-        def _(tile):
-            lanes = pl.ds(pl.multiple_of(tile * 128, 128), 128)
+        for tile in range(TILES):
+            for zc in range(NZ):
+                @pl.when(z == zc)
+                def _():
+                    for number, (_, pieces) in enumerate(steps[zc]):
+                        if pieces[tile]:
+                            pl.when(index == number)(functools.partial(take, zc, pieces[tile]))
+
+            lanes = pl.ds(tile * 128, 128)
 
             def add(segment, sums):
                 sums = list(sums)
@@ -285,11 +297,11 @@
                 return tuple(sums)
 
             zeros = tuple(jnp.zeros((8, 128), jnp.float32) for _ in range(4 * channels))
-            sums = lax.fori_loop(0, segments, add, zeros)
+            sums = lax.fori_loop(0, segments, add, zeros, unroll=4)
             for i in range(channels):
                 for o in range(2):
                     both = jnp.concatenate([sums[i * 4 + o], sums[i * 4 + 2 + o]], 0)
-                    at = pl.ds(pl.multiple_of(tile * 128 + o * bins, 128), 128)
+                    at = pl.ds(tile * 128 + o * bins, 128)
                     cross[i * 16 : (i + 1) * 16, at] = both.astype(jnp.bfloat16)
 
         result = jnp.dot(cross[...], table_ref[...], preferred_element_type=jnp.float32)
@@ -306,7 +318,7 @@
 
     def drain(zc):
         pieces = [(OWN, zc, chunk) for chunk in range(CHUNKS)]
-        pieces += [piece for taken, _ in steps[zc] for piece in taken]
+        pieces += [piece for _, tiles in steps[zc] for taken in tiles for piece in taken]
         for piece in pieces:
             for link in forwards(zc, *piece):
                 copy(link, *piece).wait_send()

time: 54.5 us -> 54.6 us (level); the launches traced: 53.7 us -> 54.5 us
  Pallas kernels: 48.9 us -> 49.7 us
    pallas_call x1, Pallas kernels: 48.9 us -> 49.7 us  [on_slice(): pl.pallas_call(slice_kernel, out_shape=jax.ShapeDtypeStruct((channels, 1,...]
where the time goes in v2:
time: 54.6 us; the launch traced here: 54.5 us
  Pallas kernels  49.7 us (91%)
  local copies, waits for them, and re-layouts  4.73 us (9%)
    pallas_call x1, Pallas kernels, on_slice(): pl.pallas_call(slice_kernel, out_shape=jax.ShapeDtypeStruct((channels, 1,...  49.7 us
    unnamed x6, local copies, waits for them, and re-layouts  2.92 us
    pallas_call x1, local copies, waits for them, and re-layouts, on_slice(): pl.pallas_call(slice_kernel, out_shape=jax.ShapeDtypeStruct((channels, 1,...  1.81 us

profile of v2, /device:TPU:0, one launch (start us, length us, event | category | flops | bytes accessed | tf_op | source)
XLA Modules:
  0.0 54.5 jit_solution(4258624298435663630)
XLA Ops:
  0.0 0.0 copy-start
  0.0 0.9 %copy-done = bf16[8,2,16,512]{3,2,1,0:T(8,128)(2,1)S(1)} copy-done((bf16[8,2,16,512]{3,2,1,0:T(8,128)(2,1)S(1)}, bf16[8,2,16,512]{3,2,1,0:T(8,128)(2,1)}, u32[]{:S(2)}) %copy-start) | copy-done | bytes 262168
  1.0 0.0 copy-start.1
  1.0 0.7 %copy-done.1 = s32[1,16]{1,0:T(1,128)S(1)} copy-done((s32[1,16]{1,0:T(1,128)S(1)}, s32[1,16]{1,0:T(1,128)}, u32[]{:S(2)}) %copy-start.1) | copy-done | bytes 88
  1.6 0.0 copy-start.2
  1.6 1.3 %copy-done.2 = bf16[1024,640]{1,0:T(8,128)(2,1)S(1)} copy-done((bf16[1024,640]{1,0:T(8,128)(2,1)S(1)}, bf16[1024,640]{1,0:T(8,128)(2,1)}, u32[]{:S(2)}) %copy-start.2) | copy-done | bytes 1310744
  2.9 49.7 %shard_map.37 = bf16[8,1,128,513]{3,2,1,0:T(8,128)(2,1)S(1)} custom-call(s32[1,16]{1,0:T(1,128)S(1)} %copy-done.1, bf16[8,2,16,512]{3,2,1,0:T(8,128)(2,1)S(1)} %copy-done, bf16[1024,640]{1,0:T(8,128)(2,1)S(1)} %copy-done.2), custom_call_target="tpu_custom_call" | custom-call | flops 1075838976 | bytes 4194304 | tf_op jit(solution)/shard_map/pallas_call | solution.py:339
  52.7 1.8 %copy.4 = bf16[8,1,128,513]{2,0,3,1:T(8,128)(2,1)} copy(bf16[8,1,128,513]{3,2,1,0:T(8,128)(2,1)S(1)} %shard_map.37) | data formatting | bytes 2101248 | tf_op jit(solution)/shard_map/pallas_call | solution.py:339
Async XLA Ops:
  0.0 0.9 %copy-start = (bf16[8,2,16,512]{3,2,1,0:T(8,128)(2,1)S(1)}, bf16[8,2,16,512]{3,2,1,0:T(8,128)(2,1)}, u32[]{:S(2)}) copy-start(bf16[8,2,16,512]{3,2,1,0:T(8,128)(2,1)} %spectra_ref.1) | copy-start | bytes 786436
  1.0 0.7 %copy-start.1 = (s32[1,16]{1,0:T(1,128)S(1)}, s32[1,16]{1,0:T(1,128)}, u32[]{:S(2)}) copy-start(s32[1,16]{1,0:T(1,128)} %partners_ref.1) | copy-start | bytes 196
  1.6 1.3 %copy-start.2 = (bf16[1024,640]{1,0:T(8,128)(2,1)S(1)}, bf16[1024,640]{1,0:T(8,128)(2,1)}, u32[]{:S(2)}) copy-start(bf16[1024,640]{1,0:T(8,128)(2,1)} %constant.2.clone.table_ref) | copy-start | bytes 3932164

commit v3 on v2

--- a/solution.py
+++ b/solution.py
@@ -14,9 +14,9 @@
 MESH = pl.DeviceIdType.MESH
 
 NZ = 4
-CHUNKS = 4
+CHUNKS = 2
 TILES = 4
-SEND_TICKS, HOP_TICKS, TAKE_TICKS, TILE_TICKS, LAG_TICKS = 15, 8, 1, 4, 4
+SEND_TICKS, HOP_TICKS, TAKE_TICKS, TILE_TICKS, LAG_TICKS = 28, 8, 1, 4, 4
 OVER_XY = {0: (0, 1), 1: (1, 2), 2: (1, 2), 3: (2, 3)}
 OWN, XCOL, YCOL, DIAG = (0, 0), (1, 0), (0, 1), (1, 1)
 
@@ -158,10 +158,10 @@
 
 
 def slice_kernel(
-    partners_ref, spectra_ref, table_ref, out_ref,
-    whole, bright, mine, mate, gathered, cross, send_sem, recv_sem, mate_send, mate_recv,
+    partners_ref, spectra_hbm, table_hbm, out_ref,
+    spectra_ref, table_ref, in_sem, whole, bright, mine, mate, gathered, cross, send_sem, recv_sem, mate_send, mate_recv,
 ):
-    channels, _, segments, bins = spectra_ref.shape
+    channels, _, segments, bins = spectra_hbm.shape
     lags = out_ref.shape[3]
     rows = segments * 2 * channels
     part = rows // CHUNKS
@@ -174,6 +174,10 @@
         "down": (grp, me - 4),
         "mate": (1 - grp, me),
     }
+    load_spectra = pltpu.make_async_copy(spectra_hbm, spectra_ref, in_sem.at[0])
+    load_table = pltpu.make_async_copy(table_hbm, table_ref, in_sem.at[1])
+    load_spectra.start()
+    load_table.start()
     lane = {"x": 0, "y": 1, "up": 2, "down": 3}
 
     barrier = pltpu.get_barrier_semaphore()
@@ -189,6 +193,7 @@
     first = lax.broadcasted_iota(jnp.int32, (bins, bins), 0)
     second = lax.broadcasted_iota(jnp.int32, (bins, bins), 1)
     band = jnp.where(jnp.abs(first - second) <= SMOOTH, 1.0, 0.0).astype(jnp.bfloat16)
+    load_spectra.wait()
     values = spectra_ref[...].astype(jnp.float32)
     power = values[:, 0] * values[:, 0] + values[:, 1] * values[:, 1]
     power = power.reshape(channels * segments, bins)
@@ -252,6 +257,7 @@
         for row in range(2 * channels):
             bright[segment, row] = jnp.broadcast_to(block[row : row + 1], (8, bins))
 
+    load_table.wait()
     steps = plan()
     factor = math.sqrt(2.0 / (bins * segments))
 
@@ -304,7 +310,8 @@
                     at = pl.ds(tile * 128 + o * bins, 128)
                     cross[i * 16 : (i + 1) * 16, at] = both.astype(jnp.bfloat16)
 
-        result = jnp.dot(cross[...], table_ref[...], preferred_element_type=jnp.float32)
+        table = table_ref[...].reshape(2 * bins, -1)
+        result = jnp.dot(cross[...], table, preferred_element_type=jnp.float32)
         result = (result * factor).astype(jnp.bfloat16)
         at = pl.ds(pl.multiple_of(pair * 16, 16), 16)
         for i in range(channels):
@@ -335,13 +342,17 @@
     wide = -(-lags // 128) * 128
     table = np.zeros((2 * bins, wide), jnp.bfloat16)
     table[:, :lags] = lag_table(bins).reshape(2 * bins, lags)
+    anywhere = pl.BlockSpec(memory_space=pl.ANY)
     vmem = pl.BlockSpec(memory_space=pltpu.VMEM)
     return pl.pallas_call(
         slice_kernel,
         out_shape=jax.ShapeDtypeStruct((channels, 1, members * channels, lags), jnp.bfloat16),
-        in_specs=[pl.BlockSpec(memory_space=pltpu.SMEM), vmem, vmem],
+        in_specs=[pl.BlockSpec(memory_space=pltpu.SMEM), anywhere, anywhere],
         out_specs=vmem,
         scratch_shapes=[
+            pltpu.VMEM(spectra.shape, jnp.bfloat16),
+            pltpu.VMEM((2 * bins // 8, 8, wide), jnp.bfloat16),
+            pltpu.SemaphoreType.DMA((2,)),
             pltpu.VMEM((bins // 128, rows, 128), jnp.float32),
             pltpu.VMEM((segments, 2 * channels, 8, bins), jnp.float32),
             pltpu.VMEM((rows, bins), jnp.bfloat16),
@@ -354,14 +365,14 @@
             pltpu.SemaphoreType.DMA((CHUNKS,)),
         ],
         compiler_params=pltpu.CompilerParams(
-            collective_id=0, has_side_effects=True, vmem_limit_bytes=48 * 2**20
+            collective_id=0, has_side_effects=True, vmem_limit_bytes=60 * 2**20
         ),
         cost_estimate=pl.CostEstimate(
             flops=2 * channels * members * channels * 2 * bins * lags,
             bytes_accessed=4 * 2**20,
             transcendentals=0,
         ),
-    )(partners, spectra, jnp.asarray(table))
+    )(partners, spectra, jnp.asarray(table.reshape(-1, 8, wide)))
 
 
 def solution(mesh):

time: 54.6 us -> 50.9 us (0.932)
  local copies, waits for them, and re-layouts: 4.73 us -> 2.75 us
  Pallas kernels: 49.7 us -> 48 us
    unnamed x6 -> x0, local copies, waits for them, and re-layouts: 2.92 us -> none
    pallas_call x1, Pallas kernels: 49.7 us -> 48 us  [on_slice(): pl.pallas_call(slice_kernel, out_shape=jax.ShapeDtypeStruct((channels, 1,...]
    pallas_call x1, local copies, waits for them, and re-layouts: 1.81 us -> 2.75 us  [on_slice(): pl.pallas_call(slice_kernel, out_shape=jax.ShapeDtypeStruct((channels, 1,...]
where the time goes in v3:
time: 50.9 us; the launch traced here: 50.8 us
  Pallas kernels  48 us (94%)
  local copies, waits for them, and re-layouts  2.75 us (5%)
    pallas_call x1, Pallas kernels, on_slice(): pl.pallas_call(slice_kernel, out_shape=jax.ShapeDtypeStruct((channels, 1,...  48 us
    pallas_call x1, local copies, waits for them, and re-layouts, on_slice(): pl.pallas_call(slice_kernel, out_shape=jax.ShapeDtypeStruct((channels, 1,...  2.75 us

profile of v3, /device:TPU:0, one launch (start us, length us, event | category | flops | bytes accessed | tf_op | source)
XLA Modules:
  0.0 50.8 jit_solution(11026077946468980200)
XLA Ops:
  0.0 48.0 %shard_map.37 = bf16[8,1,128,513]{3,2,1,0:T(8,128)(2,1)} custom-call(s32[1,16]{1,0:T(1,128)} %partners_ref.1, bf16[8,2,16,512]{3,2,1,0:T(8,128)(2,1)} %spectra_hbm.1, bf16[128,8,640]{2,1,0:T(8,128)(2,1)} %constant.2.clone.table_hbm), custom_call_target="tpu_custom_call" | custom-call | flops 1075838976 | bytes 4194304 | tf_op jit(solution)/shard_map/pallas_call | solution.py:347
  48.0 2.7 %copy.4 = bf16[8,1,128,513]{2,0,3,1:T(8,128)(2,1)} copy(bf16[8,1,128,513]{3,2,1,0:T(8,128)(2,1)} %shard_map.37) | data formatting | bytes 2101248 | tf_op jit(solution)/shard_map/pallas_call | solution.py:347

commit v4 on v3

--- a/solution.py
+++ b/solution.py
@@ -158,8 +158,8 @@
 
 
 def slice_kernel(
-    partners_ref, spectra_hbm, table_hbm, out_ref,
-    spectra_ref, table_ref, in_sem, whole, bright, mine, mate, gathered, cross, send_sem, recv_sem, mate_send, mate_recv,
+    partners_hbm, spectra_hbm, table_hbm, out_ref,
+    partners_ref, spectra_ref, table_ref, in_sem, held, out_sem, whole, bright, mine, mate, gathered, cross, send_sem, recv_sem, mate_send, mate_recv,
 ):
     channels, _, segments, bins = spectra_hbm.shape
     lags = out_ref.shape[3]
@@ -176,7 +176,9 @@
     }
     load_spectra = pltpu.make_async_copy(spectra_hbm, spectra_ref, in_sem.at[0])
     load_table = pltpu.make_async_copy(table_hbm, table_ref, in_sem.at[1])
+    load_partners = pltpu.make_async_copy(partners_hbm, partners_ref, in_sem.at[2])
     load_spectra.start()
+    load_partners.start()
     load_table.start()
     lane = {"x": 0, "y": 1, "up": 2, "down": 3}
 
@@ -193,28 +195,6 @@
     first = lax.broadcasted_iota(jnp.int32, (bins, bins), 0)
     second = lax.broadcasted_iota(jnp.int32, (bins, bins), 1)
     band = jnp.where(jnp.abs(first - second) <= SMOOTH, 1.0, 0.0).astype(jnp.bfloat16)
-    load_spectra.wait()
-    values = spectra_ref[...].astype(jnp.float32)
-    power = values[:, 0] * values[:, 0] + values[:, 1] * values[:, 1]
-    power = power.reshape(channels * segments, bins)
-    high = power.astype(jnp.bfloat16)
-    low = (power - high.astype(jnp.float32)).astype(jnp.bfloat16)
-    smooth = jnp.dot(high, band, preferred_element_type=jnp.float32)
-    smooth += jnp.dot(low, band, preferred_element_type=jnp.float32)
-    inverse = lax.rsqrt(smooth * (1.0 / (2 * SMOOTH + 1)) + FLOOR)
-    inverse = inverse.reshape(channels, segments, bins)
-    for channel in range(channels):
-        for k in range(2):
-            row = k * channels + channel
-            white = spectra_ref[channel, k].astype(jnp.float32) * inverse[channel]
-            for tile in range(bins // 128):
-                at = pl.ds(row, segments, stride=2 * channels)
-                whole[tile, at, :] = white[:, tile * 128 : (tile + 1) * 128]
-    for tile in range(bins // 128):
-        mine[:, tile * 128 : (tile + 1) * 128] = whole[tile].astype(jnp.bfloat16)
-
-    pl.semaphore_wait(barrier, 3 + jnp.where(z > 0, 1, 0) + jnp.where(z < NZ - 1, 1, 0))
-
     def to_mate(chunk):
         piece = pl.ds(chunk * part, part)
         return pltpu.make_async_remote_copy(
@@ -240,8 +220,37 @@
         for link in forwards(zc, column, plane, chunk):
             copy(link, column, plane, chunk).start()
 
+    span = segments // CHUNKS
+
+    def whiten_part(chunk):
+        now = pl.ds(chunk * span, span)
+        values = spectra_ref[:, :, now].astype(jnp.float32)
+        power = values[:, 0] * values[:, 0] + values[:, 1] * values[:, 1]
+        power = power.reshape(channels * span, bins)
+        high = power.astype(jnp.bfloat16)
+        low = (power - high.astype(jnp.float32)).astype(jnp.bfloat16)
+        smooth = jnp.dot(high, band, preferred_element_type=jnp.float32)
+        smooth += jnp.dot(low, band, preferred_element_type=jnp.float32)
+        inverse = lax.rsqrt(smooth * (1.0 / (2 * SMOOTH + 1)) + FLOOR)
+        inverse = inverse.reshape(channels, span, bins)
+        for channel in range(channels):
+            for k in range(2):
+                white = values[channel, k] * inverse[channel]
+                at = pl.ds(chunk * part + k * channels + channel, span, stride=2 * channels)
+                for tile in range(bins // 128):
+                    whole[tile, at, :] = white[:, tile * 128 : (tile + 1) * 128]
+        at = pl.ds(chunk * part, part)
+        for tile in range(bins // 128):
+            mine[at, tile * 128 : (tile + 1) * 128] = whole[tile, at].astype(jnp.bfloat16)
+
+    load_spectra.wait()
     for chunk in range(CHUNKS):
+        whiten_part(chunk)
+        if chunk == 0:
+            neighbours = 3 + jnp.where(z > 0, 1, 0) + jnp.where(z < NZ - 1, 1, 0)
+            pl.semaphore_wait(barrier, neighbours)
         to_mate(chunk).start()
+    load_partners.wait()
     other = partners_ref[0, me] % 2 == 1
     for chunk in range(CHUNKS):
         to_mate(chunk).wait_recv()
@@ -313,12 +322,18 @@
         table = table_ref[...].reshape(2 * bins, -1)
         result = jnp.dot(cross[...], table, preferred_element_type=jnp.float32)
         result = (result * factor).astype(jnp.bfloat16)
+        for i in range(channels):
+            held[pair, i] = result[i * 16 : (i + 1) * 16, :lags]
+        to_out(pair).start()
+        return packed // 8
+
+    def to_out(pair):
         at = pl.ds(pl.multiple_of(pair * 16, 16), 16)
-        for i in range(channels):
-            out_ref[i, 0, at, :] = result[i * 16 : (i + 1) * 16, :lags]
-        return packed // 8
+        return pltpu.make_async_copy(held.at[pair], out_ref.at[:, 0, at], out_sem.at[pair])
 
     lax.fori_loop(0, 2 * NZ, step, packed)
+    for pair in range(2 * NZ):
+        to_out(pair).wait()
 
     for chunk in range(CHUNKS):
         to_mate(chunk).wait_send()
@@ -342,17 +357,19 @@
     wide = -(-lags // 128) * 128
     table = np.zeros((2 * bins, wide), jnp.bfloat16)
     table[:, :lags] = lag_table(bins).reshape(2 * bins, lags)
-    anywhere = pl.BlockSpec(memory_space=pl.ANY)
-    vmem = pl.BlockSpec(memory_space=pltpu.VMEM)
+    hbm = pl.BlockSpec(memory_space=pl.ANY)
     return pl.pallas_call(
         slice_kernel,
         out_shape=jax.ShapeDtypeStruct((channels, 1, members * channels, lags), jnp.bfloat16),
-        in_specs=[pl.BlockSpec(memory_space=pltpu.SMEM), anywhere, anywhere],
-        out_specs=vmem,
+        in_specs=[hbm, hbm, hbm],
+        out_specs=hbm,
         scratch_shapes=[
+            pltpu.SMEM(partners.shape, jnp.int32),
             pltpu.VMEM(spectra.shape, jnp.bfloat16),
             pltpu.VMEM((2 * bins // 8, 8, wide), jnp.bfloat16),
-            pltpu.SemaphoreType.DMA((2,)),
+            pltpu.SemaphoreType.DMA((3,)),
+            pltpu.VMEM((members // 2, channels, 16, lags), jnp.bfloat16),
+            pltpu.SemaphoreType.DMA((members // 2,)),
             pltpu.VMEM((bins // 128, rows, 128), jnp.float32),
             pltpu.VMEM((segments, 2 * channels, 8, bins), jnp.float32),
             pltpu.VMEM((rows, bins), jnp.bfloat16),

time: 50.9 us -> 50.4 us (level)
    pallas_call x1, Pallas kernels: 48 us -> 47.5 us  [on_slice(): pl.pallas_call(slice_kernel, out_shape=jax.ShapeDtypeStruct((channels, 1,...]
where the time goes in v4:
time: 50.4 us; the launch traced here: 50.2 us
  Pallas kernels  47.5 us (94%)
  local copies, waits for them, and re-layouts  2.75 us (5%)
    pallas_call x1, Pallas kernels, on_slice(): pl.pallas_call(slice_kernel, out_shape=jax.ShapeDtypeStruct((channels, 1,...  47.5 us
    pallas_call x1, local copies, waits for them, and re-layouts, on_slice(): pl.pallas_call(slice_kernel, out_shape=jax.ShapeDtypeStruct((channels, 1,...  2.75 us

profile of v4, /device:TPU:0, one launch (start us, length us, event | category | flops | bytes accessed | tf_op | source)
XLA Modules:
  0.0 50.2 jit_solution(10076657248768903645)
XLA Ops:
  0.0 47.5 %shard_map.37 = bf16[8,1,128,513]{3,2,1,0:T(8,128)(2,1)} custom-call(s32[1,16]{1,0:T(1,128)} %partners_hbm.1, bf16[8,2,16,512]{3,2,1,0:T(8,128)(2,1)} %spectra_hbm.1, bf16[128,8,640]{2,1,0:T(8,128)(2,1)} %constant.2.clone.table_hbm), custom_call_target="tpu_custom_call" | custom-call | flops 1075838976 | bytes 4194304 | tf_op jit(solution)/shard_map/pallas_call | solution.py:361
  47.5 2.7 %copy.4 = bf16[8,1,128,513]{2,0,3,1:T(8,128)(2,1)} copy(bf16[8,1,128,513]{3,2,1,0:T(8,128)(2,1)} %shard_map.37) | data formatting | bytes 2101248 | tf_op jit(solution)/shard_map/pallas_call | solution.py:361

commit v5 on v4

--- a/solution.py
+++ b/solution.py
@@ -16,7 +16,7 @@
 NZ = 4
 CHUNKS = 2
 TILES = 4
-SEND_TICKS, HOP_TICKS, TAKE_TICKS, TILE_TICKS, LAG_TICKS = 28, 8, 1, 4, 4
+SEND_TICKS, HOP_TICKS, TAKE_TICKS, TILE_TICKS, LAG_TICKS = 28, 8, 1, 4, 6
 OVER_XY = {0: (0, 1), 1: (1, 2), 2: (1, 2), 3: (2, 3)}
 OWN, XCOL, YCOL, DIAG = (0, 0), (1, 0), (0, 1), (1, 1)
 
@@ -151,7 +151,7 @@
                 free[z] = now + TILE_TICKS
                 if tile + 1 < TILES:
                     ready[z].insert(0, (code, tile + 1))
-                else:
+                elif len(steps[z]) % 2 == 0:
                     free[z] += LAG_TICKS
         now += 1
     return steps
@@ -263,8 +263,11 @@
     def _(segment):
         block = mine[pl.ds(pl.multiple_of(segment * 2 * channels, 16), 2 * channels)]
         block = block.astype(jnp.float32)
-        for row in range(2 * channels):
-            bright[segment, row] = jnp.broadcast_to(block[row : row + 1], (8, bins))
+        both = block[:channels] + block[channels:]
+        for i in range(channels):
+            rows_of = (block[i : i + 1], block[channels + i : channels + i + 1], both[i : i + 1])
+            for place, row in enumerate(rows_of):
+                bright[segment, i * 3 + place] = jnp.broadcast_to(row, (8, bins))
 
     load_table.wait()
     steps = plan()
@@ -280,7 +283,7 @@
         number = sum(code * 8**index for index, (code, _) in enumerate(steps[zc]))
         packed = jnp.where(z == zc, number, packed)
 
-    def step(index, packed):
+    def step(index, half, packed):
         code = packed % 8
         plane, dy = code // 2, code % 2
         pair = plane * 2 + y + dy - 2 * y * dy
@@ -290,48 +293,61 @@
                 @pl.when(z == zc)
                 def _():
                     for number, (_, pieces) in enumerate(steps[zc]):
-                        if pieces[tile]:
+                        if number % 2 == half and pieces[tile]:
                             pl.when(index == number)(functools.partial(take, zc, pieces[tile]))
 
             lanes = pl.ds(tile * 128, 128)
 
-            def add(segment, sums):
-                sums = list(sums)
-                at = pl.ds(pl.multiple_of(segment * 2 * channels, 16), 2 * channels)
-                theirs = []
-                for side in range(2):
-                    block = gathered[pair * 2 + side, at, lanes].astype(jnp.float32)
-                    theirs.append((block[:channels], block[channels:]))
-                for i in range(channels):
-                    real = bright[segment, i, :, lanes]
-                    imag = bright[segment, channels + i, :, lanes]
-                    for side, (b_real, b_imag) in enumerate(theirs):
-                        at_sum = (i * 2 + side) * 2
-                        sums[at_sum] += real * b_real + imag * b_imag
-                        sums[at_sum + 1] += imag * b_real - real * b_imag
-                return tuple(sums)
-
-            zeros = tuple(jnp.zeros((8, 128), jnp.float32) for _ in range(4 * channels))
-            sums = lax.fori_loop(0, segments, add, zeros, unroll=4)
+            for low in range(0, channels, channels // 2):
+                own = range(low, low + channels // 2)
+
+                def add(segment, sums):
+                    sums = list(sums)
+                    at = pl.ds(pl.multiple_of(segment * 2 * channels, 16), 2 * channels)
+                    theirs = []
+                    for side in range(2):
+                        block = gathered[pair * 2 + side, at, lanes].astype(jnp.float32)
+                        real, imag = block[:channels], block[channels:]
+                        theirs.append((real, imag, real - imag))
+                    place = 0
+                    for i in own:
+                        ours = [bright[segment, i * 3 + k, :, lanes] for k in range(3)]
+                        for their in theirs:
+                            for k in range(3):
+                                sums[place] += ours[k] * their[k]
+                                place += 1
+                    return tuple(sums)
+
+                zeros = tuple(jnp.zeros((8, 128), jnp.float32) for _ in range(3 * channels))
+                sums = lax.fori_loop(0, segments, add, zeros, unroll=4)
+                for number, i in enumerate(own):
+                    left, right = sums[number * 6 : number * 6 + 3], sums[number * 6 + 3 : number * 6 + 6]
+                    real = [part[0] + part[1] for part in (left, right)]
+                    imag = [part[2] - part[0] + part[1] for part in (left, right)]
+                    for o, both in enumerate((real, imag)):
+                        at = pl.ds(tile * 128 + o * bins, 128)
+                        cross[half, i * 16 : (i + 1) * 16, at] = jnp.concatenate(both, 0).astype(jnp.bfloat16)
+
+        return pair
+
+    def two_steps(index, packed):
+        pairs = [step(index * 2 + half, half, packed // 8**half) for half in range(2)]
+        table = table_ref[...].reshape(2 * bins, -1)
+        left = cross[...].reshape(2 * channels * 16, 2 * bins)
+        result = jnp.dot(left, table, preferred_element_type=jnp.float32)
+        result = (result * factor).astype(jnp.bfloat16)
+        for half, pair in enumerate(pairs):
             for i in range(channels):
-                for o in range(2):
-                    both = jnp.concatenate([sums[i * 4 + o], sums[i * 4 + 2 + o]], 0)
-                    at = pl.ds(tile * 128 + o * bins, 128)
-                    cross[i * 16 : (i + 1) * 16, at] = both.astype(jnp.bfloat16)
-
-        table = table_ref[...].reshape(2 * bins, -1)
-        result = jnp.dot(cross[...], table, preferred_element_type=jnp.float32)
-        result = (result * factor).astype(jnp.bfloat16)
-        for i in range(channels):
-            held[pair, i] = result[i * 16 : (i + 1) * 16, :lags]
-        to_out(pair).start()
-        return packed // 8
+                row = (half * channels + i) * 16
+                held[pair, i] = result[row : row + 16, :lags]
+            to_out(pair).start()
+        return packed // 64
 
     def to_out(pair):
         at = pl.ds(pl.multiple_of(pair * 16, 16), 16)
         return pltpu.make_async_copy(held.at[pair], out_ref.at[:, 0, at], out_sem.at[pair])
 
-    lax.fori_loop(0, 2 * NZ, step, packed)
+    lax.fori_loop(0, NZ, two_steps, packed)
     for pair in range(2 * NZ):
         to_out(pair).wait()
 
@@ -371,11 +387,11 @@
             pltpu.VMEM((members // 2, channels, 16, lags), jnp.bfloat16),
             pltpu.SemaphoreType.DMA((members // 2,)),
             pltpu.VMEM((bins // 128, rows, 128), jnp.float32),
-            pltpu.VMEM((segments, 2 * channels, 8, bins), jnp.float32),
+            pltpu.VMEM((segments, 3 * channels, 8, bins), jnp.float32),
             pltpu.VMEM((rows, bins), jnp.bfloat16),
             pltpu.VMEM((rows, bins), jnp.bfloat16),
             pltpu.VMEM((members, rows, bins), jnp.bfloat16),
-            pltpu.VMEM((16 * channels, 2 * bins), jnp.bfloat16),
+            pltpu.VMEM((2, 16 * channels, 2 * bins), jnp.bfloat16),
             pltpu.SemaphoreType.DMA((4, members, CHUNKS)),
             pltpu.SemaphoreType.DMA((members, CHUNKS)),
             pltpu.SemaphoreType.DMA((CHUNKS,)),

time: 50.4 us -> 50.3 us (level)
  no operation moved by 1% of the time
where the time goes in v5:
time: 50.3 us; the launch traced here: 50.1 us
  Pallas kernels  47.4 us (94%)
  local copies, waits for them, and re-layouts  2.75 us (5%)
    pallas_call x1, Pallas kernels, on_slice(): pl.pallas_call(slice_kernel, out_shape=jax.ShapeDtypeStruct((channels, 1,...  47.4 us
    pallas_call x1, local copies, waits for them, and re-layouts, on_slice(): pl.pallas_call(slice_kernel, out_shape=jax.ShapeDtypeStruct((channels, 1,...  2.75 us

profile of v5, /device:TPU:0, one launch (start us, length us, event | category | flops | bytes accessed | tf_op | source)
XLA Modules:
  0.0 50.1 jit_solution(3276460330295121873)
XLA Ops:
  0.0 47.4 %shard_map.37 = bf16[8,1,128,513]{3,2,1,0:T(8,128)(2,1)} custom-call(s32[1,16]{1,0:T(1,128)} %partners_hbm.1, bf16[8,2,16,512]{3,2,1,0:T(8,128)(2,1)} %spectra_hbm.1, bf16[128,8,640]{2,1,0:T(8,128)(2,1)} %constant.2.clone.table_hbm), custom_call_target="tpu_custom_call" | custom-call | flops 1075838976 | bytes 4194304 | tf_op jit(solution)/shard_map/pallas_call | solution.py:377
  47.4 2.7 %copy.4 = bf16[8,1,128,513]{2,0,3,1:T(8,128)(2,1)} copy(bf16[8,1,128,513]{3,2,1,0:T(8,128)(2,1)} %shard_map.37) | data formatting | bytes 2101248 | tf_op jit(solution)/shard_map/pallas_call | solution.py:377

commit v6 on v5

--- a/solution.py
+++ b/solution.py
@@ -16,9 +16,15 @@
 NZ = 4
 CHUNKS = 2
 TILES = 4
-SEND_TICKS, HOP_TICKS, TAKE_TICKS, TILE_TICKS, LAG_TICKS = 28, 8, 1, 4, 6
-OVER_XY = {0: (0, 1), 1: (1, 2), 2: (1, 2), 3: (2, 3)}
+SEND_TICKS, HOP_TICKS, TAKE_TICKS, TILE_TICKS, LAG_TICKS = 31, 8, 1, 4, 6
 OWN, XCOL, YCOL, DIAG = (0, 0), (1, 0), (0, 1), (1, 1)
+LINKS = {"x": "x", "y": "y", "u": "up", "d": "down"}
+SOURCES = {
+    0: {XCOL: "xx xx dx xx", YCOL: "yy yy yd yy", DIAG: "yx xy yx dd"},
+    1: {XCOL: "uu xx xx dx", YCOL: "uu yy yy yd", DIAG: "uy yx dd xy"},
+    2: {XCOL: "ux xx xx dd", YCOL: "yu yy yy dd", DIAG: "xy uu yx dy"},
+    3: {XCOL: "xx ux xx xx", YCOL: "yy yu yy yy", DIAG: "uu yx xy yx"},
+}
 
 
 def from_partner(array, axis, distance):
@@ -78,25 +84,23 @@
     return jnp.stack(outputs, 1)
 
 
+def source(z, column, plane, chunk):
+    if column == OWN:
+        return "down" if plane > z else "up" if plane < z else None
+    return LINKS[SOURCES[z][column].split()[plane][chunk]]
+
+
 def forwards(z, column, plane, chunk):
+    dx, dy = column
     links = []
-    if column == OWN:
-        if plane >= z and z > 0:
-            links.append("down")
-        if plane <= z and z < NZ - 1:
-            links.append("up")
-        links += ["x", "y"]
-    elif column == XCOL:
-        if plane in OVER_XY[z] and chunk < CHUNKS // 2:
-            links.append("y")
-    elif column == YCOL:
-        if plane in OVER_XY[z] and chunk >= CHUNKS // 2:
-            links.append("x")
-    else:
-        if z > 0 and plane >= z and plane not in OVER_XY[z - 1]:
-            links.append("down")
-        if z < NZ - 1 and plane <= z and plane not in OVER_XY[z + 1]:
-            links.append("up")
+    if z > 0 and source(z - 1, column, plane, chunk) == "down":
+        links.append("down")
+    if z < NZ - 1 and source(z + 1, column, plane, chunk) == "up":
+        links.append("up")
+    if dx == 0 and source(z, (1, dy), plane, chunk) == "x":
+        links.append("x")
+    if dy == 0 and source(z, (dx, 1), plane, chunk) == "y":
+        links.append("y")
     return links
 
 

time: 50.3 us -> 45.6 us (0.907)
  Pallas kernels: 47.4 us -> 42.7 us
    pallas_call x1, Pallas kernels: 47.4 us -> 42.7 us  [on_slice(): pl.pallas_call(slice_kernel, out_shape=jax.ShapeDtypeStruct((channels, 1,...]
where the time goes in v6:
time: 45.6 us; the launch traced here: 45.5 us
  Pallas kernels  42.7 us (94%)
  local copies, waits for them, and re-layouts  2.75 us (6%)
    pallas_call x1, Pallas kernels, on_slice(): pl.pallas_call(slice_kernel, out_shape=jax.ShapeDtypeStruct((channels, 1,...  42.7 us
    pallas_call x1, local copies, waits for them, and re-layouts, on_slice(): pl.pallas_call(slice_kernel, out_shape=jax.ShapeDtypeStruct((channels, 1,...  2.75 us

profile of v6, /device:TPU:0, one launch (start us, length us, event | category | flops | bytes accessed | tf_op | source)
XLA Modules:
  0.0 45.5 jit_solution(10006160488689994154)
XLA Ops:
  0.0 42.7 %shard_map.37 = bf16[8,1,128,513]{3,2,1,0:T(8,128)(2,1)} custom-call(s32[1,16]{1,0:T(1,128)} %partners_hbm.1, bf16[8,2,16,512]{3,2,1,0:T(8,128)(2,1)} %spectra_hbm.1, bf16[128,8,640]{2,1,0:T(8,128)(2,1)} %constant.2.clone.table_hbm), custom_call_target="tpu_custom_call" | custom-call | flops 1075838976 | bytes 4194304 | tf_op jit(solution)/shard_map/pallas_call | solution.py:381
  42.7 2.7 %copy.4 = bf16[8,1,128,513]{2,0,3,1:T(8,128)(2,1)} copy(bf16[8,1,128,513]{3,2,1,0:T(8,128)(2,1)} %shard_map.37) | data formatting | bytes 2101248 | tf_op jit(solution)/shard_map/pallas_call | solution.py:381

commit v7 on v6

--- a/solution.py
+++ b/solution.py
@@ -20,10 +20,10 @@
 OWN, XCOL, YCOL, DIAG = (0, 0), (1, 0), (0, 1), (1, 1)
 LINKS = {"x": "x", "y": "y", "u": "up", "d": "down"}
 SOURCES = {
-    0: {XCOL: "xx xx dx xx", YCOL: "yy yy yd yy", DIAG: "yx xy yx dd"},
-    1: {XCOL: "uu xx xx dx", YCOL: "uu yy yy yd", DIAG: "uy yx dd xy"},
-    2: {XCOL: "ux xx xx dd", YCOL: "yu yy yy dd", DIAG: "xy uu yx dy"},
-    3: {XCOL: "xx ux xx xx", YCOL: "yy yu yy yy", DIAG: "uu yx xy yx"},
+    0: {XCOL: "xx xx dx dx", YCOL: "yy yy yd yd", DIAG: "yx yx xy xy"},
+    1: {XCOL: "xx xx xx dx", YCOL: "yy yy yy yd", DIAG: "uu xy dd xy"},
+    2: {XCOL: "ux xx xx xx", YCOL: "yu yy yy yy", DIAG: "xy uu xy dd"},
+    3: {XCOL: "ux ux xx xx", YCOL: "yu yu yy yy", DIAG: "xy xy yx yx"},
 }
 
 

time: 45.6 us -> 45.4 us (level)
  no operation moved by 1% of the time
where the time goes in v7:
time: 45.4 us; the launch traced here: 45.3 us
  Pallas kernels  42.5 us (94%)
  local copies, waits for them, and re-layouts  2.75 us (6%)
    pallas_call x1, Pallas kernels, on_slice(): pl.pallas_call(slice_kernel, out_shape=jax.ShapeDtypeStruct((channels, 1,...  42.5 us
    pallas_call x1, local copies, waits for them, and re-layouts, on_slice(): pl.pallas_call(slice_kernel, out_shape=jax.ShapeDtypeStruct((channels, 1,...  2.75 us

profile of v7, /device:TPU:0, one launch (start us, length us, event | category | flops | bytes accessed | tf_op | source)
XLA Modules:
  0.0 45.3 jit_solution(9405539955590768723)
XLA Ops:
  0.0 42.5 %shard_map.37 = bf16[8,1,128,513]{3,2,1,0:T(8,128)(2,1)} custom-call(s32[1,16]{1,0:T(1,128)} %partners_hbm.1, bf16[8,2,16,512]{3,2,1,0:T(8,128)(2,1)} %spectra_hbm.1, bf16[128,8,640]{2,1,0:T(8,128)(2,1)} %constant.2.clone.table_hbm), custom_call_target="tpu_custom_call" | custom-call | flops 1075838976 | bytes 4194304 | tf_op jit(solution)/shard_map/pallas_call | solution.py:381
  42.5 2.7 %copy.4 = bf16[8,1,128,513]{2,0,3,1:T(8,128)(2,1)} copy(bf16[8,1,128,513]{3,2,1,0:T(8,128)(2,1)} %shard_map.37) | data formatting | bytes 2101248 | tf_op jit(solution)/shard_map/pallas_call | solution.py:381

commit v8 on v7

--- a/solution.py
+++ b/solution.py
@@ -227,8 +227,7 @@
     span = segments // CHUNKS
 
     def whiten_part(chunk):
-        now = pl.ds(chunk * span, span)
-        values = spectra_ref[:, :, now].astype(jnp.float32)
+        values = spectra_ref[...].astype(jnp.float32)[:, :, chunk * span : (chunk + 1) * span]
         power = values[:, 0] * values[:, 0] + values[:, 1] * values[:, 1]
         power = power.reshape(channels * span, bins)
         high = power.astype(jnp.bfloat16)

time: 45.4 us -> 45.4 us (level)
  no operation moved by 1% of the time
where the time goes in v8:
time: 45.4 us; the launch traced here: 45.3 us
  Pallas kernels  42.5 us (94%)
  local copies, waits for them, and re-layouts  2.75 us (6%)
    pallas_call x1, Pallas kernels, on_slice(): pl.pallas_call(slice_kernel, out_shape=jax.ShapeDtypeStruct((channels, 1,...  42.5 us
    pallas_call x1, local copies, waits for them, and re-layouts, on_slice(): pl.pallas_call(slice_kernel, out_shape=jax.ShapeDtypeStruct((channels, 1,...  2.75 us

profile of v8, /device:TPU:0, one launch (start us, length us, event | category | flops | bytes accessed | tf_op | source)
XLA Modules:
  0.0 45.3 jit_solution(9405539955590768723)
XLA Ops:
  0.0 42.5 %shard_map.37 = bf16[8,1,128,513]{3,2,1,0:T(8,128)(2,1)} custom-call(s32[1,16]{1,0:T(1,128)} %partners_hbm.1, bf16[8,2,16,512]{3,2,1,0:T(8,128)(2,1)} %spectra_hbm.1, bf16[128,8,640]{2,1,0:T(8,128)(2,1)} %constant.2.clone.table_hbm), custom_call_target="tpu_custom_call" | custom-call | flops 1075838976 | bytes 4194304 | tf_op jit(solution)/shard_map/pallas_call | solution.py:380
  42.5 2.7 %copy.4 = bf16[8,1,128,513]{2,0,3,1:T(8,128)(2,1)} copy(bf16[8,1,128,513]{3,2,1,0:T(8,128)(2,1)} %shard_map.37) | data formatting | bytes 2101248 | tf_op jit(solution)/shard_map/pallas_call | solution.py:380
